TPU v7x, 256 devices: a whole 4x4x8 slice. The times are simulated.
256 devices in a mesh: sq: 16 (over x, y), sk: 16 (over z, core).
Axes of the slice: x: 4, y: 4, z: 8, core: 2. Of those that a mesh axis runs over, the one named last changes fastest.
Arguments:
- video: bfloat16 [49152, 3072], P(('sq', 'sk')), may hold values from -6 to 6
- assign: int32 [49152], P(('sq', 'sk')), may hold values from 0 to 12287, as said below
- qkv_weight: bfloat16 [3072, 6144], P(None, 'sq'), may hold values from -0.109375 to 0.109375
- qk_gain: float32 [2, 128], replicated, may hold values from 1.5 to 2.5
- text_kv: bfloat16 [2, 256, 2048], P(None, None, 'sq')
- out_weight: bfloat16 [2048, 3072], P('sq'), may hold values from -0.125 to 0.125
Outputs:
- mixed: bfloat16 [49152, 3072], P(('sq', 'sk'))
Inputs may be any that keep to these rules, and one draw needn't show every extreme that they name: `assign`: A video token of device index i*16+j of sq+sk merges into a token held by a device of the same j, merged token m being held by device m // 48. At most 24 of one device's tokens go to the tokens of one index of sq; in every draw each device sends exactly 24 to one of them. Merged tokens may have no video token.
All inputs are finite; a program needn't handle non-finite values.
Results may differ from a plain program's by a relative error of at most 0.01.
Values may be sent and summed in bfloat16 or wider, within the bound.
No kernel may reach another device: no remote copies, remote signals or barrier semaphores. Data moves between devices by JAX's collectives and lax.ppermute only.
A program may use at most 128 MiB of HBM per device.

v0:
```python
import math

import jax
import jax.numpy as jnp
from jax import lax
from jax.sharding import PartitionSpec as P


def rms_norm(values, gain):
    return values * lax.rsqrt(jnp.mean(values * values, axis=-1, keepdims=True) + 1e-06) * gain


def absorb(running, queries, key_block, value_block, score_scale):
    maxima, totals, accum = running
    scores = (
        jnp.einsum("qhd,khd->hqk", queries, key_block, preferred_element_type=jnp.float32)
        * score_scale
    )
    raised = jnp.maximum(maxima, jnp.max(scores, axis=-1))
    fading = jnp.exp(maxima - raised)
    probs = jnp.exp(scores - raised[:, :, None])
    totals = totals * fading + jnp.sum(probs, axis=-1)
    update = jnp.einsum(
        "hqk,khd->qhd", probs.astype(jnp.bfloat16), value_block, preferred_element_type=jnp.float32
    )
    accum = accum * jnp.transpose(fading)[:, :, None] + update
    return (raised, totals, accum)


def per_device(video, assign, qkv_weight, qk_gain, text_kv, out_weight):
    src_rows, model_width = video.shape
    sq_count = lax.axis_size("sq")
    sk_count = lax.axis_size("sk")
    slot_cap = 2 * src_rows // sq_count
    merged_dev = src_rows // 4
    head_size = qk_gain.shape[1]
    heads_here = qkv_weight.shape[1] // (3 * head_size)
    owner_dev = assign // merged_dev
    peer_index = owner_dev // sk_count
    local_id = assign % merged_dev
    peer_hot = (peer_index[:, None] == jnp.arange(sq_count, dtype=jnp.int32)[None, :]).astype(
        jnp.int32
    )
    slot_rank = jnp.sum((jnp.cumsum(peer_hot, axis=0) - 1) * peer_hot, axis=1)
    position = peer_index * slot_cap + slot_rank
    send_rows = jnp.zeros((sq_count * slot_cap, model_width), jnp.bfloat16).at[position].set(video)
    send_ids = (
        jnp.full((sq_count * slot_cap,), -1.0, jnp.float32)
        .at[position]
        .set(local_id.astype(jnp.float32))
    )
    got_rows, got_ids = (
        lax.all_to_all(
            send_rows.reshape(sq_count, slot_cap, model_width),
            "sq",
            split_axis=0,
            concat_axis=0,
            tiled=True,
        ),
        lax.all_to_all(
            send_ids.astype(jnp.bfloat16).reshape(sq_count, slot_cap),
            "sq",
            split_axis=0,
            concat_axis=0,
            tiled=True,
        ),
    )
    flat_rows = got_rows.reshape(sq_count * slot_cap, model_width)
    flat_ids = got_ids.reshape(sq_count * slot_cap).astype(jnp.float32)
    member = (flat_ids[:, None] == jnp.arange(merged_dev, dtype=jnp.float32)[None, :]).astype(
        jnp.bfloat16
    )
    row_totals = lax.dot_general(
        member, flat_rows, (((0,), (0,)), ((), ())), preferred_element_type=jnp.float32
    )
    counts = jnp.sum(member.astype(jnp.float32), axis=0)
    merged = (row_totals / jnp.maximum(counts, 1.0)[:, None]).astype(jnp.bfloat16)
    projected = jnp.dot(
        lax.all_gather(merged, "sq", axis=0, tiled=True),
        qkv_weight,
        preferred_element_type=jnp.float32,
    )
    group_rows = projected.shape[0]
    projected = projected.reshape(group_rows, heads_here, 3, head_size)
    queries = rms_norm(projected[:, :, 0], qk_gain[0]).astype(jnp.bfloat16)
    key_rows = rms_norm(projected[:, :, 1], qk_gain[1]).astype(jnp.bfloat16)
    value_rows = projected[:, :, 2].astype(jnp.bfloat16)
    score_scale = 1.0 / math.sqrt(head_size)
    text_keys = text_kv[0].reshape(text_kv.shape[1], heads_here, head_size)
    text_values = text_kv[1].reshape(text_kv.shape[1], heads_here, head_size)
    starting = (
        jnp.full((heads_here, group_rows), -jnp.inf, jnp.float32),
        jnp.zeros((heads_here, group_rows), jnp.float32),
        jnp.zeros((group_rows, heads_here, head_size), jnp.float32),
    )
    starting = absorb(starting, queries, text_keys, text_values, score_scale)
    cycle_keys = key_rows.reshape(group_rows, heads_here * head_size)
    cycle_values = value_rows.reshape(group_rows, heads_here * head_size)
    key_part = lax.all_gather(cycle_keys, "sk", axis=0, tiled=True)
    value_part = lax.all_gather(cycle_values, "sk", axis=0, tiled=True)
    amount = key_part.shape[0]
    span = 1024
    steps_total = amount // span
    key_blocks = key_part.reshape(steps_total, span, heads_here, head_size)
    value_blocks = value_part.reshape(steps_total, span, heads_here, head_size)

    def one_step(index, state):
        return absorb(state, queries, key_blocks[index], value_blocks[index], score_scale)

    maxima, totals, accum = lax.fori_loop(0, steps_total, one_step, starting)
    attended = (
        (accum / jnp.transpose(totals)[:, :, None])
        .astype(jnp.bfloat16)
        .reshape(group_rows, heads_here * head_size)
    )
    own_rows = lax.all_to_all(attended, "sq", split_axis=0, concat_axis=1, tiled=True)
    group_width = heads_here * head_size
    all_weights = lax.all_gather(out_weight, "sq", axis=0, tiled=True)
    groups_all = all_weights.shape[0] // group_width
    columns = own_rows.reshape(merged_dev, groups_all, group_width)
    partials = jnp.einsum(
        "mgc,gcd->gmd",
        columns,
        all_weights.reshape(groups_all, group_width, model_width),
        preferred_element_type=jnp.float32,
    ).astype(jnp.bfloat16)
    delta = jnp.sum(partials.astype(jnp.float32), axis=0)
    delta_rows = delta.astype(jnp.bfloat16)
    back_send = jnp.dot(member, delta_rows, preferred_element_type=jnp.float32).astype(jnp.bfloat16)
    got_back = lax.all_to_all(
        back_send.reshape(sq_count, slot_cap, model_width),
        "sq",
        split_axis=0,
        concat_axis=0,
        tiled=True,
    )
    got_back = got_back.reshape(sq_count * slot_cap, model_width)
    return (video.astype(jnp.float32) + got_back[position].astype(jnp.float32)).astype(jnp.bfloat16)


def solution(mesh):
    in_specs = (
        P(("sq", "sk"), None),
        P(("sq", "sk")),
        P(None, "sq"),
        P(),
        P(None, None, "sq"),
        P("sq", None),
    )
    out_specs = P(("sq", "sk"), None)
    return jax.shard_map(
        per_device, mesh=mesh, in_specs=in_specs, out_specs=out_specs, check_vma=False
    )
```

profile of v0, /device:TPU:32, one launch (start us, length us, event | category | flops | bytes accessed | tf_op | source)
XLA Modules:
  0.0 372.1 jit_solution(6325636260525825562)
XLA Ops:
  6.5 0.8 fusion.51
  7.4 0.6 reduce-window.6
  8.4 1.2 scatter_custom_fusion
  9.6 0.7 all_to_all.31
  10.3 7.0 %all-to-all-start = ((bf16[16,1,24]{2,1,0:T(2,128)(2,1)}), bf16[16,1,24]{2,1,0:T(2,128)(2,1)S(1)}, u32[]{:S(2)}, u32[]{:S(2)}) async-start(bf16[16,1,24]{2,1,0:T(2,128)(2,1)} %all_to_all.31), calls=%async_computation | async-start | bytes 16384 | tf_op jit(solution)/shard_map/all_to_all | solution.py:60
  17.3 4.7 %scatter_custom_fusion.1 = bf16[384,3072]{1,0:T(8,128)(2,1)} fusion(s32[192]{0:T(256)S(1)} %compare_select_fusion, bf16[192,3072]{1,0:T(8,128)(2,1)} %param.8, bf16[]{:T(256)} %constant.100.clone.1), kind=kCustom, calls=%fused_computation.35 | custom fusion | bytes 2359808 | tf_op jit(solution)/shard_map/scatter | solution.py:46
  22.0 2.8 all-to-all-done
  24.8 4.5 %all-to-all-start.1 = ((bf16[16,24,3072]{2,1,0:T(8,128)(2,1)}), bf16[16,24,3072]{2,1,0:T(8,128)(2,1)}, u32[]{:S(2)}, u32[]{:S(2)}) async-start(bf16[16,24,3072]{2,1,0:T(8,128)(2,1)} %bitcast.103), calls=%async_computation.1 | async-start | bytes 4718592 | tf_op jit(solution)/shard_map/all_to_all | solution.py:53
  29.6 32.3 %all-to-all-done.1 = bf16[16,24,3072]{2,1,0:T(8,128)(2,1)} async-done(((bf16[16,24,3072]{2,1,0:T(8,128)(2,1)}), bf16[16,24,3072]{2,1,0:T(8,128)(2,1)}, u32[]{:S(2)}, u32[]{:S(2)}) %all-to-all-start.1) | async-done | bytes 2359328 | tf_op jit(solution)/shard_map/all_to_all | solution.py:53
  61.9 2.9 fusion.22
  64.9 58.6 %all-gather.6.cloned.1.call-done = bf16[768,3072]{1,0:T(8,128)(2,1)} async-done(((bf16[48,3072]{1,0:T(8,128)(2,1)}), bf16[768,3072]{1,0:T(8,128)(2,1)}) %all-gather.6.cloned.1.call-update) | async-done | bytes 4718608 | tf_op jit(solution)/shard_map/all_gather | solution.py:79
  123.6 4.4 %fusion.56 = f32[768,384]{0,1:T(8,128)S(1)} fusion(bf16[768,3072]{1,0:T(8,128)(2,1)} %all-gather.6.cloned.1.call-done, bf16[3072,384]{1,0:T(8,128)(2,1)S(1)} %copy-done), kind=kOutput, calls=%fused_computation.97 | convolution fusion | flops 1811939328 | bytes 8257536 | tf_op jit(solution)/shard_map/dot_general | solution.py:78
  128.0 0.9 copy-done.2
  129.3 0.8 fusion.32
  130.2 1.0 slice.50
  131.3 0.8 copy.42
  133.1 1.2 fusion.55
  134.4 1.9 fusion.25
  136.3 1.2 copy.36
  137.6 1.2 fusion.35
  138.8 32.0 %all-gather.8.cloned.1.call-done = bf16[12288,128]{1,0:T(8,128)(2,1)} async-done(((bf16[768,128]{1,0:T(8,128)(2,1)}), bf16[12288,128]{1,0:T(8,128)(2,1)}) %all-gather.8.cloned.1.call-update) | async-done | bytes 3145744 | tf_op jit(solution)/shard_map/all_gather | solution.py:99
  170.8 41.5 %all-gather.12.cloned.1.call-done = bf16[12288,1,1,128]{3,0,2,1:T(8,128)(2,1)} async-done(((bf16[768,1,1,128]{3,0,2,1:T(8,128)(2,1)}), bf16[12288,1,1,128]{3,0,2,1:T(8,128)(2,1)}) %all-gather.12.cloned.1.call-update) | async-done | bytes 3145744 | tf_op jit(solution)/shard_map/all_gather | solution.py:100
  212.2 46.3 %while.17 = (s32[]{:T(128)}, f32[1,768]{1,0:T(1,128)S(1)}, f32[1,768]{1,0:T(1,128)S(1)}, f32[768,1,128]{0,2,1:T(8,128)S(1)}, bf16[12,1024,1,128]{3,1,2,0:T(8,128...) while((s32[]{:T(128)}, f32[1,768]{1,0:T(1,128)S(1)}, ...), condition=%wide.region_13.14_spmd, body=%wide.region_10.13_spmd.sunk | while | flops 409143552 | bytes 10997845 | solution.py:110
  212.2 1.5 multiply_reduce_fusion.3
  213.8 1.7 fusion.71
  215.5 0.6 fusion.70
  216.1 1.5 multiply_reduce_fusion.3
  217.7 1.7 fusion.71
  219.3 0.6 fusion.70
  219.9 1.5 multiply_reduce_fusion.3
  221.5 1.7 fusion.71
  223.2 0.6 fusion.70
  223.8 1.5 multiply_reduce_fusion.3
  225.4 1.7 fusion.71
  227.7 1.6 multiply_reduce_fusion.3
  229.3 1.7 fusion.71
  230.9 0.6 fusion.70
  231.5 1.5 multiply_reduce_fusion.3
  233.1 1.7 fusion.71
  234.8 0.6 fusion.70
  235.4 1.5 multiply_reduce_fusion.3
  237.0 1.7 fusion.71
  239.3 1.5 multiply_reduce_fusion.3
  240.8 1.7 fusion.71
  242.5 0.6 fusion.70
  243.1 1.5 multiply_reduce_fusion.3
  244.7 1.7 fusion.71
  246.4 0.6 fusion.70
  247.0 1.5 multiply_reduce_fusion.3
  248.5 1.7 fusion.71
  250.2 0.6 fusion.70
  250.8 1.5 multiply_reduce_fusion.3
  252.4 1.7 fusion.71
  254.1 0.6 fusion.70
  254.7 1.6 multiply_reduce_fusion.3
  256.3 1.7 fusion.71
  259.0 17.0 %all_to_all.36 = bf16[16,48,128]{2,1,0:T(8,128)(2,1)S(1)} all-to-all(bf16[16,48,128]{2,1,0:T(8,128)(2,1)S(1)} %bitcast.107), channel_id=1, replica_groups=mesh['sq'=16,'sk'=16] {'sq'}, dimensions={0} | all-to-all | bytes 393216 | tf_op jit(solution)/shard_map/all_to_all | solution.py:116
  275.9 34.8 %all-gather.10.cloned.1.call-done = bf16[2048,3072]{1,0:T(8,128)(2,1)} async-done(((bf16[128,3072]{1,0:T(8,128)(2,1)}), bf16[2048,3072]{1,0:T(8,128)(2,1)}) %all-gather.10.cloned.1.call-update) | async-done | bytes 12582928 | tf_op jit(solution)/shard_map/all_gather | solution.py:118
  310.7 6.4 %fusion.23 = bf16[48,3072]{1,0:T(8,128)(2,1)S(1)} fusion(bf16[16,128,3072]{2,1,0:T(8,128)(2,1)} %bitcast.102, bf16[16,48,128]{2,1,0:T(8,128)(2,1)S(1)} %all_to_all.36), kind=kOutput, calls=%fused_computation.30 | convolution fusion | flops 608550912 | bytes 13074432 | tf_op jit(solution)/shard_map/mgc,gcd->gmd/dot_general | solution.py:121
  317.0 2.2 convolution_convert_fusion.1
  319.3 5.4 %all-to-all-start.3 = ((bf16[16,24,3072]{2,1,0:T(8,128)(2,1)}), bf16[16,24,3072]{2,1,0:T(8,128)(2,1)}, u32[]{:S(2)}, u32[]{:S(2)}) async-start(bf16[16,24,3072]{2,1,0:T(8,128)(2,1)} %bitcast.104), calls=%async_computation.3 | async-start | bytes 4718592 | tf_op jit(solution)/shard_map/all_to_all | solution.py:130
  324.7 33.7 %all-to-all-done.3 = bf16[16,24,3072]{2,1,0:T(8,128)(2,1)} async-done(((bf16[16,24,3072]{2,1,0:T(8,128)(2,1)}), bf16[16,24,3072]{2,1,0:T(8,128)(2,1)}, u32[]{:S(2)}, u32[]{:S(2)}) %all-to-all-start.3) | async-done | bytes 2359328 | tf_op jit(solution)/shard_map/all_to_all | solution.py:130
  358.4 4.5 %gather_fusion = bf16[192,3072]{1,0:T(8,128)(2,1)S(1)} fusion(bf16[384,3072]{1,0:T(8,128)(2,1)} %bitcast.27, s32[1024]{0:T(1024)S(1)} %pad_clamp_fusion), kind=kCustom, calls=%fused_computation | custom fusion | bytes 2360064 | tf_op jit(solution)/shard_map/gather | solution.py:138
  362.9 2.7 add_convert_fusion
  (89 shorter events, 4.8 us)
Async XLA Ops:
  6.5 117.0 %copy-start = (bf16[3072,384]{1,0:T(8,128)(2,1)S(1)}, bf16[3072,384]{1,0:T(8,128)(2,1)}, u32[]{:S(2)}) copy-start(bf16[3072,384]{1,0:T(8,128)(2,1)} %param.10) | copy-start | bytes 7077892
  8.3 16.5 %copy-start.4 = (s32[192]{0:T(256)}, s32[192]{0:T(256)S(1)}, u32[]{:S(2)}) copy-start(s32[192]{0:T(256)S(1)} %compare_select_fusion) | copy-start | bytes 2308
  10.3 14.5 %all-to-all-start = ((bf16[16,1,24]{2,1,0:T(2,128)(2,1)}), bf16[16,1,24]{2,1,0:T(2,128)(2,1)S(1)}, u32[]{:S(2)}, u32[]{:S(2)}) async-start(bf16[16,1,24]{2,1,0:T(2,128)(2,1)} %all_to_all.31), calls=%async_computation | async-start | bytes 16384 | tf_op jit(solution)/shard_map/all_to_all | solution.py:60
  24.8 37.1 %all-to-all-start.1 = ((bf16[16,24,3072]{2,1,0:T(8,128)(2,1)}), bf16[16,24,3072]{2,1,0:T(8,128)(2,1)}, u32[]{:S(2)}, u32[]{:S(2)}) async-start(bf16[16,24,3072]{2,1,0:T(8,128)(2,1)} %bitcast.103), calls=%async_computation.1 | async-start | bytes 4718592 | tf_op jit(solution)/shard_map/all_to_all | solution.py:53
  29.3 35.6 %copy-start.6 = (f32[2,128]{1,0:T(2,128)S(1)}, f32[2,128]{1,0:T(2,128)}, u32[]{:S(2)}) copy-start(f32[2,128]{1,0:T(2,128)} %param.11) | copy-start | bytes 3076
  29.3 94.3 %all-gather.6.cloned.1.call-start = ((), (), s32[]{:S(2)}) async-start(), calls=%async_computation.4 | async-start | bytes 5013504 | tf_op jit(solution)/shard_map/all_gather | solution.py:79
  64.8 105.9 %all-gather.8.cloned.1.call-start = ((), (), s32[]{:S(2)}) async-start(), calls=%async_computation.5 | async-start | bytes 3342336 | tf_op jit(solution)/shard_map/all_gather | solution.py:99
  64.9 68.2 %copy-start.3 = (f32[128]{0:T(128)}, f32[128]{0:T(128)S(1)}, u32[]{:S(2)}) copy-start(f32[128]{0:T(128)S(1)} %get-tuple-element.182) | copy-start | bytes 1540
  127.9 1.0 copy-start.2
  130.2 82.1 %all-gather.12.cloned.1.call-start = ((), (), s32[]{:S(2)}) async-start(), calls=%async_computation.7 | async-start | bytes 3342336 | tf_op jit(solution)/shard_map/all_gather | solution.py:100
  132.1 178.6 %all-gather.10.cloned.1.call-start = ((), (), s32[]{:S(2)}) async-start(), calls=%async_computation.6 | async-start | bytes 13369344 | tf_op jit(solution)/shard_map/all_gather | solution.py:118
  132.9 1.5 copy-start.1
  319.3 5.4 %copy-start.5 = (s32[192]{0:T(256)S(1)}, s32[192]{0:T(256)}, u32[]{:S(2)}) copy-start(s32[192]{0:T(256)} %copy-done.4) | copy-start | bytes 2308
  319.3 39.2 %all-to-all-start.3 = ((bf16[16,24,3072]{2,1,0:T(8,128)(2,1)}), bf16[16,24,3072]{2,1,0:T(8,128)(2,1)}, u32[]{:S(2)}, u32[]{:S(2)}) async-start(bf16[16,24,3072]{2,1,0:T(8,128)(2,1)} %bitcast.104), calls=%async_computation.3 | async-start | bytes 4718592 | tf_op jit(solution)/shard_map/all_to_all | solution.py:130
Sparse Core Ops, SparseCore 0:
  65.0 58.5 all-gather.5
  130.3 40.4 all-gather.7
  172.6 39.5 all-gather.11
  214.6 96.0 all-gather.9
where the time goes:
time: 374 us; the launch traced here: 372 us
  waiting for transfers between devices  236 us (63%)
  matrix products  57.5 us (15%)
  starting transfers between devices  17.1 us (5%)
  blocking collectives  17 us (5%)
  local copies, waits for them, and re-layouts  15.9 us (4%)
  other arithmetic  14.4 us (4%)
  between operations  13.5 us (4%)
    all_gather x1, waiting for transfers between devices, per_device(): lax.all_gather(merged, 'sq', axis=0, tiled=True)  58.6 us
    all_gather x1, waiting for transfers between devices, per_device(): value_part = lax.all_gather(cycle_values, 'sk', axis=0, tiled=True)  41.5 us
    all_gather x1, waiting for transfers between devices, per_device(): all_weights = lax.all_gather(out_weight, 'sq', axis=0, tiled=True)  34.8 us
    all_to_all x1, waiting for transfers between devices, per_device(): lax.all_to_all(back_send.reshape(sq_count, slot_cap, model_width), 'sq',...  33.7 us
    all_to_all x1, waiting for transfers between devices, per_device(): lax.all_to_all(send_rows.reshape(sq_count, slot_cap, model_width), 'sq',...  32.3 us
    all_gather x1, waiting for transfers between devices, per_device(): key_part = lax.all_gather(cycle_keys, 'sk', axis=0, tiled=True)  32 us
    dot_general x13, matrix products, absorb(): jnp.einsum('hqk,khd->qhd', probs.astype(jnp.bfloat16), value_block, prefe...  22 us
    dot_general x13, matrix products, absorb(): jnp.einsum('qhd,khd->hqk', queries, key_block, preferred_element_type=jnp...  19.7 us
  transfers between devices with their start and end apart: 7, of which 7 were waited for; matrix products, arithmetic and copies ran while one was open for 16% of the time, Pallas kernels for 0%

commit v1 on v0

v1 whole, which is shorter than its diff:
```python
import functools
import math

import jax
import jax.numpy as jnp
from jax import lax
from jax.experimental import pallas as pl
from jax.experimental.pallas import tpu as pltpu
from jax.sharding import Mesh, PartitionSpec as P

BF = jnp.bfloat16
F32 = jnp.float32
HD = 128
SQ = 16
SK = 16
CAP = 24
MRG = 48
SRC = 192
ROWS = SQ * MRG
TEXT = 256
D = 3072


def dot(a, b):
    return lax.dot_general(a, b, (((1,), (0,)), ((), ())), preferred_element_type=F32)


def dot_t(a, b):
    return lax.dot_general(a, b, (((1,), (1,)), ((), ())), preferred_element_type=F32)


def pack_kernel(row_ref, col_ref, video_ref, out_ref):
    peer_row = row_ref[...] // (MRG * SK)
    peer_col = col_ref[...] // (MRG * SK)
    before = lax.broadcasted_iota(jnp.int32, (SRC, SRC), 0) < lax.broadcasted_iota(
        jnp.int32, (SRC, SRC), 1
    )
    same = jnp.where(before & (peer_row == peer_col), 1.0, 0.0)
    rank = jnp.sum(same, axis=0, keepdims=True).astype(jnp.int32)
    position = peer_row * CAP + rank
    slots = lax.broadcasted_iota(jnp.int32, (SQ * CAP, SRC), 0)
    hot = jnp.where(slots == position, 1.0, 0.0).astype(BF)
    out_ref[...] = dot(hot, video_ref[...]).astype(BF)


def pack_rows(assign, video):
    width = 768
    return pl.pallas_call(
        pack_kernel,
        grid=(D // width,),
        in_specs=[
            pl.BlockSpec((1, SRC), lambda c: (0, 0)),
            pl.BlockSpec((SRC, 1), lambda c: (0, 0)),
            pl.BlockSpec((SRC, width), lambda c: (0, c)),
        ],
        out_specs=pl.BlockSpec((SQ * CAP, width), lambda c: (0, c)),
        out_shape=jax.ShapeDtypeStruct((SQ * CAP, D), BF),
        compiler_params=pltpu.CompilerParams(vmem_limit_bytes=32 << 20),
        name="pack_rows",
    )(assign.reshape(1, SRC), assign.reshape(SRC, 1), video)


def project_kernel(rows_ref, weight_ref, gain_ref, q_ref, kv_ref):
    full = dot(rows_ref[...], weight_ref[...])

    def norm(part, gain):
        return part * lax.rsqrt(jnp.mean(part * part, axis=-1, keepdims=True) + 1e-06) * gain

    factor = math.log2(math.e) / math.sqrt(HD)
    q_ref[...] = (norm(full[:, :HD], gain_ref[0:1, :]) * factor).astype(BF)
    kv_ref[:, :HD] = norm(full[:, HD : 2 * HD], gain_ref[1:2, :]).astype(BF)
    kv_ref[:, HD:] = full[:, 2 * HD :].astype(BF)


def project(rows, weight, gain):
    count = rows.shape[0]
    step = 128
    return pl.pallas_call(
        project_kernel,
        grid=(count // step,),
        in_specs=[
            pl.BlockSpec((step, D), lambda r: (r, 0)),
            pl.BlockSpec((D, 3 * HD), lambda r: (0, 0)),
            pl.BlockSpec((2, HD), lambda r: (0, 0)),
        ],
        out_specs=[
            pl.BlockSpec((step, HD), lambda r: (r, 0)),
            pl.BlockSpec((step, 2 * HD), lambda r: (r, 0)),
        ],
        out_shape=[
            jax.ShapeDtypeStruct((count, HD), BF),
            jax.ShapeDtypeStruct((count, 2 * HD), BF),
        ],
        compiler_params=pltpu.CompilerParams(vmem_limit_bytes=32 << 20),
        name="project",
    )(rows, weight, gain)


QB = 256


def absorb(q_ref, m_ref, l_ref, acc_ref, keys, values, first):
    for block in range(ROWS // QB):
        span = pl.ds(block * QB, QB)
        scores = dot_t(q_ref[span, :], keys)
        top = jnp.max(scores, axis=-1, keepdims=True)
        if first:
            raised = top
        else:
            before = m_ref[span, :1]
            raised = jnp.maximum(before, top)
            fading = jnp.exp2(before - raised)
        probs = jnp.exp2(scores - raised)
        total = jnp.sum(probs, axis=-1, keepdims=True)
        update = dot(probs.astype(BF), values)
        if first:
            l_ref[span, :] = jnp.broadcast_to(total, (QB, HD))
            acc_ref[span, :] = update
        else:
            l_ref[span, :] = l_ref[span, :] * fading + total
            acc_ref[span, :] = acc_ref[span, :] * fading + update
        m_ref[span, :] = jnp.broadcast_to(raised, (QB, HD))


def attend_kernel(need_ref, q_ref, text_ref, kv_ref, out_ref, m_ref, l_ref, acc_ref, done_ref):
    step = pl.program_id(0)

    @pl.when(step == 0)
    def _():
        absorb(q_ref, m_ref, l_ref, acc_ref, text_ref[0], text_ref[1], True)

    chunk = 768

    for part in range(kv_ref.shape[0] // chunk):
        span = pl.ds(part * chunk, chunk)
        absorb(q_ref, m_ref, l_ref, acc_ref, kv_ref[span, :HD], kv_ref[span, HD:], False)

    @pl.when(step == pl.num_programs(0) - 1)
    def _():
        done_ref[...] = (acc_ref[...] / l_ref[...]).astype(BF)
        attended = done_ref[...]
        for peer in range(SQ):
            hot = jnp.where(
                lax.broadcasted_iota(jnp.int32, (SRC, ROWS), 1) == need_ref[peer], 1.0, 0.0
            ).astype(BF)
            out_ref[peer] = dot(hot, attended).astype(BF)


def attend(need, queries, text, kv):
    step = 1536
    return pl.pallas_call(
        attend_kernel,
        grid=(kv.shape[0] // step,),
        in_specs=[
            pl.BlockSpec((SQ, SRC, 1), lambda k: (0, 0, 0)),
            pl.BlockSpec((ROWS, HD), lambda k: (0, 0)),
            pl.BlockSpec((2, TEXT, HD), lambda k: (0, 0, 0)),
            pl.BlockSpec((step, 2 * HD), lambda k: (k, 0)),
        ],
        out_specs=pl.BlockSpec((SQ, SRC, HD), lambda k: (0, 0, 0)),
        out_shape=jax.ShapeDtypeStruct((SQ, SRC, HD), BF),
        scratch_shapes=[
            pltpu.VMEM((ROWS, HD), F32),
            pltpu.VMEM((ROWS, HD), F32),
            pltpu.VMEM((ROWS, HD), F32),
            pltpu.VMEM((ROWS, HD), BF),
        ],
        compiler_params=pltpu.CompilerParams(vmem_limit_bytes=48 << 20),
        name="attend",
    )(need, queries, text, kv)


def finish_kernel(core_ref, parts_ref, own_ref, other_ref, video_ref, out_ref, flat_ref):
    step = pl.program_id(0)
    half = pl.num_programs(0) // 2

    @pl.when(step == 0)
    def _():
        for group in range(SQ):
            flat_ref[:, group * HD : (group + 1) * HD] = parts_ref[group]

    def product(weight_ref):
        delta = dot(flat_ref[...], weight_ref[...]).astype(BF).astype(F32)
        out_ref[...] = (video_ref[...].astype(F32) + delta).astype(BF)

    @pl.when(step < half)
    def _():
        product(own_ref)

    @pl.when(step >= half)
    def _():
        product(other_ref)


def finish(core, parts, own, other, video):
    width = 512
    half = D // 2 // width

    def place(step, core_ref):
        return (0, lax.rem(step + half * core_ref[0], 2 * half))

    return pl.pallas_call(
        finish_kernel,
        grid_spec=pltpu.PrefetchScalarGridSpec(
            num_scalar_prefetch=1,
            grid=(2 * half,),
            in_specs=[
                pl.BlockSpec((SQ, SRC, HD), lambda c, core_ref: (0, 0, 0)),
                pl.BlockSpec((SQ * HD, width), lambda c, core_ref: (0, jnp.minimum(c, half - 1))),
                pl.BlockSpec((SQ * HD, width), lambda c, core_ref: (0, jnp.maximum(c - half, 0))),
                pl.BlockSpec((SRC, width), place),
            ],
            out_specs=pl.BlockSpec((SRC, width), place),
            scratch_shapes=[pltpu.VMEM((SRC, SQ * HD), BF)],
        ),
        out_shape=jax.ShapeDtypeStruct((SRC, D), BF),
        compiler_params=pltpu.CompilerParams(vmem_limit_bytes=32 << 20),
        name="finish",
    )(core, parts, own, other, video)


def member_of(all_assign, mine):
    peers = all_assign // (MRG * SK)
    local = (all_assign % MRG).astype(F32)
    chosen = (peers == mine).astype(F32)
    triangle = jnp.triu(jnp.ones((SRC, SRC), F32), 1)
    rank = dot(chosen.astype(BF), triangle.astype(BF))
    slots = jnp.arange(CAP, dtype=F32)
    placed = jnp.where(rank[:, None, :] == slots[None, :, None], chosen[:, None, :], 0.0)
    ids = jnp.sum(placed * (local + 1.0)[:, None, :], axis=2) - 1.0
    flat = ids.reshape(SQ * CAP)
    return (jnp.arange(MRG, dtype=F32)[:, None] == flat[None, :]).astype(BF)


def per_device(video, assign, qkv_weight, qk_gain, text_kv, out_weight):
    mine = lax.axis_index(("x", "y"))
    core = lax.axis_index("c")
    all_assign = lax.all_gather(assign.reshape(1, SRC), ("x", "y"), axis=0, tiled=True)
    half_weight = lax.dynamic_slice_in_dim(out_weight, core * (D // 2), D // 2, 1)
    own_half = lax.all_gather(half_weight, ("x", "y"), axis=0, tiled=True)

    send = pack_rows(assign, video).reshape(SQ, CAP, D)
    got = lax.all_to_all(send, ("x", "y"), split_axis=0, concat_axis=0, tiled=True)
    member = member_of(all_assign, mine)
    need = (all_assign // (MRG * SK)) * MRG + all_assign % MRG
    counts = jnp.sum(member.astype(F32), axis=1)
    totals = dot(member, got.reshape(SQ * CAP, D))
    merged = (totals / jnp.maximum(counts, 1.0)[:, None]).astype(BF)

    merged, own_half = lax.optimization_barrier((merged, own_half))
    rows = lax.all_gather(merged, ("x", "y"), axis=0, tiled=True)
    other_half = lax.ppermute(own_half, "c", [(0, 1), (1, 0)])
    queries, kv = project(rows, qkv_weight, qk_gain)
    all_kv = lax.all_gather(kv, ("z", "c"), axis=0, tiled=True)
    parts = attend(need.reshape(SQ, SRC, 1), queries, text_kv, all_kv)
    parts = lax.all_to_all(parts, ("x", "y"), split_axis=0, concat_axis=0, tiled=True)
    return finish(core.astype(jnp.int32).reshape(1), parts, own_half, other_half, video)


def solution(mesh):
    fine = Mesh(mesh.devices.reshape(4, 4, 8, 2), ("x", "y", "z", "c"))
    sq = ("x", "y")
    in_specs = (
        P(("x", "y", "z", "c"), None),
        P(("x", "y", "z", "c")),
        P(None, sq),
        P(),
        P(None, None, sq),
        P(sq, None),
    )
    out_specs = P(("x", "y", "z", "c"), None)
    return jax.shard_map(
        per_device, mesh=fine, in_specs=in_specs, out_specs=out_specs, check_vma=False
    )
```

time: 374 us -> 305 us (0.82)
  waiting for transfers between devices: 236 us -> 117 us
  blocking collectives: 17 us -> 98.7 us
  matrix products: 57.5 us -> 3.04 us
  Pallas kernels: 0 us -> 46.3 us
  other arithmetic: 14.4 us -> 0.33 us
  local copies, waits for them, and re-layouts: 15.9 us -> 11.5 us
    unnamed x0 -> x1, blocking collectives: none -> 98.7 us
    all_gather x4 -> x3, waiting for transfers between devices: 167 us -> 102 us  [the longest x1 56.6 us: per_device(): rows = lax.all_gather(merged, ('x', 'y'), axis=0, tiled=True)]
    dot_general x30 -> x2, matrix products: 57.5 us -> 3.04 us  [dot(): lax.dot_general(a, b, (((1,), (0,)), ((), ())), preferred_element_type=F32)]
    all_to_all x3 -> x2, waiting for transfers between devices: 68.8 us -> 15 us  [the longest x1 15 us: per_device(): lax.all_to_all(parts, ('x', 'y'), split_axis=0, concat_axis=0, tiled=True)]
    pallas_call x0 -> x4, Pallas kernels: none -> 46.3 us  [the longest x1 30.7 us: attend(): pl.pallas_call(attend_kernel, grid=(kv.shape[0] // step,), in_specs=[pl.B...]
    all_to_all x1 -> x0, blocking collectives: 17 us -> none  [per_device(): lax.all_to_all(attended, 'sq', split_axis=0, concat_axis=1, tiled=True)]
    reduce_sum x17 -> x2, other arithmetic: 7.39 us -> 0.27 us  [the longest x1 0.15 us: member_of(): ids = jnp.sum(placed * (local + 1.0)[:, None, :], axis=2) - 1.0]
    unnamed x17 -> x25, local copies, waits for them, and re-layouts: 2.11 us -> 9.09 us
  transfers between devices with their start and end apart: 7 -> 6, of which waited for: 7 -> 3; matrix products, arithmetic and copies ran while one was open for 16% -> 2% of each run, Pallas kernels for 0% -> 11%
where the time goes in v1:
time: 305 us
  waiting for transfers between devices  117 us (38%)
  blocking collectives  98.7 us (32%)
  Pallas kernels  46.3 us (15%)
  starting transfers between devices  14.3 us (5%)
  between operations  13.9 us (5%)
  local copies, waits for them, and re-layouts  11.5 us (4%)
    unnamed x1, blocking collectives  98.7 us
    all_gather x1, waiting for transfers between devices, per_device(): rows = lax.all_gather(merged, ('x', 'y'), axis=0, tiled=True)  56.6 us
    all_gather x1, waiting for transfers between devices, per_device(): all_kv = lax.all_gather(kv, ('z', 'c'), axis=0, tiled=True)  44.9 us
    pallas_call x1, Pallas kernels, attend(): pl.pallas_call(attend_kernel, grid=(kv.shape[0] // step,), in_specs=[pl.B...  30.7 us
    all_to_all x1, waiting for transfers between devices, per_device(): lax.all_to_all(parts, ('x', 'y'), split_axis=0, concat_axis=0, tiled=True)  15 us
    unnamed x25, local copies, waits for them, and re-layouts  9.09 us
    pallas_call x1, Pallas kernels, finish(): pl.pallas_call(finish_kernel, grid_spec=pltpu.PrefetchScalarGridSpec(num_...  7.86 us
    all_to_all x1, starting transfers between devices, per_device(): lax.all_to_all(send, ('x', 'y'), split_axis=0, concat_axis=0, tiled=True)  7.21 us
  transfers between devices with their start and end apart: 6, of which 3 were waited for; matrix products, arithmetic and copies ran while one was open for 2% of the time, Pallas kernels for 11%

profile of v1, /device:TPU:32, one launch (start us, length us, event | category | flops | bytes accessed | tf_op | source)
XLA Modules:
  0.0 304.8 jit_solution(12912225435654037349)
XLA Ops:
  6.5 0.0 copy-start
  6.5 0.0 all-gather.5.cloned.1.call-start
  6.5 1.1 copy-done
  7.7 0.8 constant_dynamic-slice_fusion
  8.4 0.0 all-gather.5.cloned.1.call-update
  8.5 0.8 copy.9.col_ref
  9.3 0.0 copy-start.2
  9.3 1.3 copy-done.2
  10.5 0.0 copy-start.7
  10.5 0.7 copy-done.7
  11.2 3.2 %pack_rows.1 = bf16[384,3072]{1,0:T(8,128)(2,1)} custom-call(s32[1,192]{1,0:T(1,128)S(1)} %bitcast.10, s32[192,1]{1,0:T(8,128)S(1)} %copy.9.col_ref, bf16[192,3072]{1,0:T(8,128)(2,1)S(1)} %copy-done.2), custom_call_target="tpu_custom_call" | custom-call | tf_op jit(solution)/shard_map/pack_rows/pallas_call | solution.py:48
  14.4 0.0 copy-start.10
  14.4 0.0 copy-start.8
  14.4 7.2 %all-to-all-start = ((bf16[16,24,3072]{2,1,0:T(8,128)(2,1)}), bf16[16,24,3072]{2,1,0:T(8,128)(2,1)}, u32[]{:S(2)}, u32[]{:S(2)}) async-start(bf16[16,24,3072]{2,1,0:T(8,128)(2,1)} %bitcast.5), calls=%async_computation | async-start | bytes 4718592 | tf_op jit(solution)/shard_map/all_to_all | solution.py:243
  21.6 0.0 copy-start.5
  21.6 0.0 copy-start.9
  21.6 0.0 all-gather.7.cloned.1.call-start
  21.7 0.0 copy-done.10
  21.7 0.6 dynamic-slice
  22.9 0.0 copy-done.8
  22.9 0.3 dynamic-update-slice
  23.2 98.7 %all-reduce = s32[3072]{0:T(1024)S(1)} all-reduce(s32[3072]{0:T(1024)S(1)} %dynamic-update-slice), channel_id=2, replica_groups=mesh['x'=4,'y'=4,'z'=8,'c'=2] {'x','y'}, use_global_device_ids=true, to_apply=%add | all-reduce | flops 3072 | bytes 24576
  122.0 0.1 reshape.50
  122.1 0.1 reshape.45
  122.2 0.1 reshape.43
  122.3 0.1 fusion.1
  122.4 0.1 multiply_reduce_fusion
  122.6 0.1 sub.16
  122.7 0.1 convert_reduce_fusion
  122.8 0.0 all-to-all-done
  122.8 2.9 fusion
  125.7 0.0 all-gather.5.cloned.1.call-done.own_ref
  125.7 0.0 copy-start.6
  125.7 0.0 all-gather.7.cloned.1.call-update
  125.7 0.0 all-gather.9.cloned.1.call-start
  125.8 56.6 %all-gather.7.cloned.1.call-done.rows_ref = bf16[768,3072]{1,0:T(8,128)(2,1)} async-done(((bf16[48,3072]{1,0:T(8,128)(2,1)}), bf16[768,3072]{1,0:T(8,128)(2,1)}) %all-gather.7.cloned.1.call-update) | async-done | bytes 4718608 | tf_op jit(solution)/shard_map/all_gather | solution.py:251
  182.4 0.0 copy-done.5
  182.4 0.0 copy-done.9
  182.4 0.0 copy-start.4
  182.4 2.3 copy-done.4
  184.8 4.6 %project.1 = (bf16[768,128]{1,0:T(8,128)(2,1)S(1)}, bf16[768,256]{1,0:T(8,128)(2,1)}) custom-call(bf16[768,3072]{1,0:T(8,128)(2,1)S(1)} %copy-done.4, bf16[3072,384]{1,0:T(8,128)(2,1)S(1)} %copy-done.5, f32[2,128]{1,0:T(2,128)S(1)} %copy-done.9), custom_call_target="tpu_custom_call" | custom-call | tf_op jit(solution)/shard_map/project/pallas_call | solution.py:78
  189.4 0.0 all-gather.9.cloned.1.call-update
  189.4 0.1 collective-permute-start
  189.6 0.5 copy.10.need_ref
  190.1 44.9 %all-gather.9.cloned.1.call-done.kv_ref = bf16[12288,256]{1,0:T(8,128)(2,1)} async-done(((bf16[768,256]{1,0:T(8,128)(2,1)}), bf16[12288,256]{1,0:T(8,128)(2,1)}) %all-gather.9.cloned.1.call-update) | async-done | bytes 6291472 | tf_op jit(solution)/shard_map/all_gather | solution.py:254
  235.0 0.0 copy-done.6
  235.0 30.7 %attend.1 = bf16[16,192,128]{2,1,0:T(8,128)(2,1)} custom-call(s32[16,192,1]{2,1,0:T(8,128)S(1)} %copy.10.need_ref, bf16[768,128]{1,0:T(8,128)(2,1)S(1)} %get-tuple-element.10.q_ref, bf16[2,256,128]{2,1,0:T(8,128)(2,1)S(1)} %copy-done.6, bf16[12288,256]{1,0:T(8,128)(2,1)} %all-gather.9.cloned.1.call-done.kv_ref), custom_call_target="tpu_custom_call" | custom-call | tf_op jit(solution)/shard_map/attend/pallas_call | solution.py:151
  265.7 0.0 copy-start.3
  265.7 6.9 %all-to-all-start.1 = ((bf16[16,192,128]{2,1,0:T(8,128)(2,1)}), bf16[16,192,128]{2,1,0:T(8,128)(2,1)S(1)}, u32[]{:S(2)}, u32[]{:S(2)}) async-start(bf16[16,192,128]{2,1,0:T(8,128)(2,1)} %attend.1), calls=%async_computation.1 | async-start | bytes 1572864 | tf_op jit(solution)/shard_map/all_to_all | solution.py:256
  272.6 0.0 collective-permute-done.other_ref
  272.6 15.0 %all-to-all-done.1.parts_ref = bf16[16,192,128]{2,1,0:T(8,128)(2,1)S(1)} async-done(((bf16[16,192,128]{2,1,0:T(8,128)(2,1)}), bf16[16,192,128]{2,1,0:T(8,128)(2,1)S(1)}, u32[]{:S(2)}, u32[]{:S(2)}) %all-to-all-start.1) | async-done | bytes 786464 | tf_op jit(solution)/shard_map/all_to_all | solution.py:256
  287.7 0.0 copy-done.3
  287.7 0.0 copy-start.1
  287.7 2.8 copy-done.1
  290.4 7.9 %finish.1 = bf16[192,3072]{1,0:T(8,128)(2,1)} custom-call(s32[1]{0:T(128)} %bitcast.core_ref, bf16[16,192,128]{2,1,0:T(8,128)(2,1)S(1)} %all-to-all-done.1.parts_ref, bf16[2048,1536]{1,0:T(8,128)(2,1)S(1)} %copy-done.1, bf16[2048,1536]{1,0:T(8,128)(2,1)} %collective-permute-done.other_ref, bf16[192,3072]{1,0:T(8,128)(2,1)S(1)} %copy-done.3), custom_call_target="tpu_custom_call" | custom-call | tf_op jit(solution)/shard_map/finish/pallas_call | solution.py:202
  (8 shorter events, 0.1 us)
Async XLA Ops:
  6.5 1.1 copy-start
  6.5 119.2 %all-gather.5.cloned.1.call-start = ((), (), s32[]{:S(2)}) async-start(), calls=%async_computation.2 | async-start | bytes 6684672 | tf_op jit(solution)/shard_map/all_gather | solution.py:240
  9.3 1.3 copy-start.2
  10.5 0.7 copy-start.7
  14.4 7.3 %copy-start.10 = (u32[256]{0:T(256)S(1)}, u32[256]{0:T(256)}, u32[]{:S(2)}) copy-start(u32[256]{0:T(256)} %constant.64) | copy-start | bytes 3076
  14.4 8.5 %copy-start.8 = (s32[192]{0:T(256)S(1)}, s32[192]{0:T(256)}, u32[]{:S(2)}) copy-start(s32[192]{0:T(256)} %param.7) | copy-start | bytes 2308
  14.4 108.4 %all-to-all-start = ((bf16[16,24,3072]{2,1,0:T(8,128)(2,1)}), bf16[16,24,3072]{2,1,0:T(8,128)(2,1)}, u32[]{:S(2)}, u32[]{:S(2)}) async-start(bf16[16,24,3072]{2,1,0:T(8,128)(2,1)} %bitcast.5), calls=%async_computation | async-start | bytes 4718592 | tf_op jit(solution)/shard_map/all_to_all | solution.py:243
  21.6 160.8 %copy-start.5 = (bf16[3072,384]{1,0:T(8,128)(2,1)S(1)}, bf16[3072,384]{1,0:T(8,128)(2,1)}, u32[]{:S(2)}) copy-start(bf16[3072,384]{1,0:T(8,128)(2,1)} %weight_ref.1) | copy-start | bytes 7077892
  21.6 160.8 %copy-start.9 = (f32[2,128]{1,0:T(2,128)S(1)}, f32[2,128]{1,0:T(2,128)}, u32[]{:S(2)}) copy-start(f32[2,128]{1,0:T(2,128)} %gain_ref.1) | copy-start | bytes 3076
  21.6 160.8 %all-gather.7.cloned.1.call-start = ((), (), s32[]{:S(2)}) async-start(), calls=%async_computation.3 | async-start | bytes 5013504 | tf_op jit(solution)/shard_map/all_gather | solution.py:251
  125.7 109.3 %copy-start.6 = (bf16[2,256,128]{2,1,0:T(8,128)(2,1)S(1)}, bf16[2,256,128]{2,1,0:T(8,128)(2,1)}, u32[]{:S(2)}) copy-start(bf16[2,256,128]{2,1,0:T(8,128)(2,1)} %text_ref.1) | copy-start | bytes 393220
  125.7 109.3 %all-gather.9.cloned.1.call-start = ((), (), s32[]{:S(2)}) async-start(), calls=%async_computation.4 | async-start | bytes 6684672 | tf_op jit(solution)/shard_map/all_gather | solution.py:254
  182.4 2.3 copy-start.4
  189.4 83.2 %collective-permute-start = (bf16[2048,1536]{1,0:T(8,128)(2,1)}, bf16[2048,1536]{1,0:T(8,128)(2,1)}, u32[]{:S(2)}, u32[]{:S(2)}) collective-permute-start(bf16[2048,1536]{1,0:T(8,128)(2,1)} %all-gather.5.cloned.1.call-done.own_ref), channel_id=1, source_target_pairs={{0,1},{1,0},{2,3},{3,2},{4,5},{5,4},{6,7},{7,6},{8,9},{9,8},{10,11... | collective-permute-start | bytes 18874376 | tf_op jit(solution)/shard_map/ppermute | solution.py:252
  265.7 22.0 %copy-start.3 = (bf16[192,3072]{1,0:T(8,128)(2,1)S(1)}, bf16[192,3072]{1,0:T(8,128)(2,1)}, u32[]{:S(2)}) copy-start(bf16[192,3072]{1,0:T(8,128)(2,1)} %video_ref.3) | copy-start | bytes 3538948
  265.7 22.0 %all-to-all-start.1 = ((bf16[16,192,128]{2,1,0:T(8,128)(2,1)}), bf16[16,192,128]{2,1,0:T(8,128)(2,1)S(1)}, u32[]{:S(2)}, u32[]{:S(2)}) async-start(bf16[16,192,128]{2,1,0:T(8,128)(2,1)} %attend.1), calls=%async_computation.1 | async-start | bytes 1572864 | tf_op jit(solution)/shard_map/all_to_all | solution.py:256
  287.7 2.8 copy-start.1
Sparse Core Ops, SparseCore 0:
  9.8 92.1 all-gather.4
  125.9 56.5 all-gather.6
  189.6 45.4 all-gather.8
